TPU v7x, 256 devices: a whole 4x4x8 slice. The times are simulated.
256 devices in a mesh: seq: 32 (over z, y), head: 8 (over x, core).
Axes of the slice: x: 4, y: 4, z: 8, core: 2. Of those that a mesh axis runs over, the one named last changes fastest.
Arguments:
- lin_query: bfloat16 [32768, 8192], P('seq', 'head'), may hold values from -6 to 6
- lin_key: bfloat16 [32768, 8192], P('seq', 'head'), may hold values from -6 to 6
- lin_value: bfloat16 [32768, 8192], P('seq', 'head'), may hold values from -6 to 6
- log_decay: float32 [32768, 64], P('seq', 'head'), may hold values from 0 to 0.54, as said below
- norm_gain: float32 [8192], P('head'), may hold values from 0.5 to 1.5
Outputs:
- lin_out: bfloat16 [32768, 8192], P(('seq', 'head'))
Inputs may be any that keep to these rules, and one draw needn't show every extreme that they name: `log_decay`: nonnegative decay exponents.
All inputs are finite; a program needn't handle non-finite values.
Results may differ from a plain program's by a relative error of at most 0.001.
Values may be sent and summed in bfloat16 or wider, within the bound.
A program may use at most 128 MiB of HBM per device.

v0:
```python
import jax
import jax.numpy as jnp
from jax import lax
from jax.sharding import PartitionSpec as P

HD = 128


THREE_PASS = lax.Precision.HIGH


def from_behind(block, axis, distance):
    devices = range(lax.axis_size(axis))
    route = [(i - distance, i) for i in devices if i - distance in devices]
    return lax.ppermute(block, axis, route)


def on_device(lin_query, lin_key, lin_value, log_decay, norm_gain):
    row_count = lin_query.shape[0]
    head_count = norm_gain.shape[0] // HD
    query_heads = lin_query.reshape(row_count, head_count, HD)
    key_heads = lin_key.reshape(row_count, head_count, HD)
    value_heads = lin_value.reshape(row_count, head_count, HD)
    cumulative = jnp.cumsum(log_decay, axis=0)
    ending = cumulative[-1]
    scaled_keys = (
        key_heads.astype(jnp.float32) * jnp.exp(-(ending[None, :] - cumulative))[:, :, None]
    )
    local_state = jnp.einsum(
        "shd,she->hde",
        scaled_keys,
        value_heads,
        precision=THREE_PASS,
        preferred_element_type=jnp.float32,
    )
    group_decay = jnp.exp(-ending)
    empty_state = jnp.zeros_like(local_state)

    def relay_step(index, received):
        return from_behind(received * group_decay[:, None, None] + local_state, "seq", 1)

    incoming = lax.fori_loop(0, lax.axis_size("seq") - 1, relay_step, empty_state)
    block_rows = min(512, row_count)
    pieces = []
    for block_index in range(row_count // block_rows):
        first_row = block_index * block_rows
        last_row = first_row + block_rows
        scores = jnp.einsum(
            "thd,shd->hts",
            query_heads[first_row:last_row],
            key_heads[:last_row],
            preferred_element_type=jnp.float32,
        )
        distance = (
            cumulative[first_row:last_row].T[:, :, None] - cumulative[:last_row].T[:, None, :]
        )
        causal = jnp.arange(first_row, last_row)[:, None] >= jnp.arange(last_row)[None, :]
        weights = jnp.where(causal[None], jnp.exp(-jnp.maximum(distance, 0.0)), 0.0) * scores
        pieces.append(
            jnp.einsum(
                "hts,shd->thd",
                weights,
                value_heads[:last_row],
                precision=THREE_PASS,
                preferred_element_type=jnp.float32,
            )
        )
    within = jnp.concatenate(pieces, axis=0)
    decayed_queries = query_heads.astype(jnp.float32) * jnp.exp(-cumulative)[:, :, None]
    carried = jnp.einsum(
        "thd,hde->the",
        decayed_queries,
        incoming,
        precision=THREE_PASS,
        preferred_element_type=jnp.float32,
    )
    combined = within + carried
    normed = (
        combined
        * lax.rsqrt(jnp.mean(combined * combined, axis=-1, keepdims=True) + 1e-06)
        * norm_gain.reshape(head_count, HD)
    )
    head_rows = normed.reshape(row_count, head_count * HD).astype(jnp.bfloat16)
    return lax.all_to_all(head_rows, "head", split_axis=0, concat_axis=1, tiled=True)


def solution(mesh):
    in_specs = (P("seq", "head"), P("seq", "head"), P("seq", "head"), P("seq", "head"), P("head"))
    out_specs = P(("seq", "head"), None)
    return jax.shard_map(
        on_device, mesh=mesh, in_specs=in_specs, out_specs=out_specs, check_vma=False
    )
```

profile of v0, /device:TPU:128, one launch (start us, length us, event | category | flops | bytes accessed | tf_op | source)
XLA Modules:
  0.0 622.5 jit_solution(2154876907227921101)
XLA Ops:
  51.3 522.4 %while.10 = (s32[]{:T(128)}, f32[8,128,128]{2,1,0:T(8,128)S(1)}, f32[8]{0:T(128)S(1)}, f32[8,128,128]{2,1,0:T(8,128)S(1)}, s32[]{:T(128)}) while((s32[]{:T(128)}, f32[8,128,128]{2,1,0:T(8,128)S(1)}, f32[8]{0:T(128)S(1)}, f32[8,128,128]{2,1,0:T(8,128)S(1)}, s32[]{:T(128)}) %tuple.24), condition=%wide.region_3.4_spmd, body=%wide.region_2.3_spmd.sunk | while | flops 262146 | bytes 3670149 | solution.py:42
  54.9 15.4 %collective-permute-done = f32[8,128,128]{2,1,0:T(8,128)S(1)} collective-permute-done((f32[8,128,128]{2,1,0:T(8,128)S(1)}, f32[8,128,128]{2,1,0:T(8,128)S(1)}, u32[]{:S(2)}, u32[]{:S(2)}) %collective-permute-start) | collective-permute-done | bytes 524320 | tf_op jit(solution)/shard_map/while/body/eval_jaxpr/ppermute | solution.py:15
  72.3 16.1 %collective-permute-done = f32[8,128,128]{2,1,0:T(8,128)S(1)} collective-permute-done((f32[8,128,128]{2,1,0:T(8,128)S(1)}, f32[8,128,128]{2,1,0:T(8,128)S(1)}, u32[]{:S(2)}, u32[]{:S(2)}) %collective-permute-start) | collective-permute-done | bytes 524320 | tf_op jit(solution)/shard_map/while/body/eval_jaxpr/ppermute | solution.py:15
  90.5 15.2 %collective-permute-done = f32[8,128,128]{2,1,0:T(8,128)S(1)} collective-permute-done((f32[8,128,128]{2,1,0:T(8,128)S(1)}, f32[8,128,128]{2,1,0:T(8,128)S(1)}, u32[]{:S(2)}, u32[]{:S(2)}) %collective-permute-start) | collective-permute-done | bytes 524320 | tf_op jit(solution)/shard_map/while/body/eval_jaxpr/ppermute | solution.py:15
  107.7 14.2 %collective-permute-done = f32[8,128,128]{2,1,0:T(8,128)S(1)} collective-permute-done((f32[8,128,128]{2,1,0:T(8,128)S(1)}, f32[8,128,128]{2,1,0:T(8,128)S(1)}, u32[]{:S(2)}, u32[]{:S(2)}) %collective-permute-start) | collective-permute-done | bytes 524320 | tf_op jit(solution)/shard_map/while/body/eval_jaxpr/ppermute | solution.py:15
  124.0 13.3 %collective-permute-done = f32[8,128,128]{2,1,0:T(8,128)S(1)} collective-permute-done((f32[8,128,128]{2,1,0:T(8,128)S(1)}, f32[8,128,128]{2,1,0:T(8,128)S(1)}, u32[]{:S(2)}, u32[]{:S(2)}) %collective-permute-start) | collective-permute-done | bytes 524320 | tf_op jit(solution)/shard_map/while/body/eval_jaxpr/ppermute | solution.py:15
  139.3 12.5 %collective-permute-done = f32[8,128,128]{2,1,0:T(8,128)S(1)} collective-permute-done((f32[8,128,128]{2,1,0:T(8,128)S(1)}, f32[8,128,128]{2,1,0:T(8,128)S(1)}, u32[]{:S(2)}, u32[]{:S(2)}) %collective-permute-start) | collective-permute-done | bytes 524320 | tf_op jit(solution)/shard_map/while/body/eval_jaxpr/ppermute | solution.py:15
  153.8 12.5 %collective-permute-done = f32[8,128,128]{2,1,0:T(8,128)S(1)} collective-permute-done((f32[8,128,128]{2,1,0:T(8,128)S(1)}, f32[8,128,128]{2,1,0:T(8,128)S(1)}, u32[]{:S(2)}, u32[]{:S(2)}) %collective-permute-start) | collective-permute-done | bytes 524320 | tf_op jit(solution)/shard_map/while/body/eval_jaxpr/ppermute | solution.py:15
  168.4 12.6 %collective-permute-done = f32[8,128,128]{2,1,0:T(8,128)S(1)} collective-permute-done((f32[8,128,128]{2,1,0:T(8,128)S(1)}, f32[8,128,128]{2,1,0:T(8,128)S(1)}, u32[]{:S(2)}, u32[]{:S(2)}) %collective-permute-start) | collective-permute-done | bytes 524320 | tf_op jit(solution)/shard_map/while/body/eval_jaxpr/ppermute | solution.py:15
  183.0 13.7 %collective-permute-done = f32[8,128,128]{2,1,0:T(8,128)S(1)} collective-permute-done((f32[8,128,128]{2,1,0:T(8,128)S(1)}, f32[8,128,128]{2,1,0:T(8,128)S(1)}, u32[]{:S(2)}, u32[]{:S(2)}) %collective-permute-start) | collective-permute-done | bytes 524320 | tf_op jit(solution)/shard_map/while/body/eval_jaxpr/ppermute | solution.py:15
  198.8 14.8 %collective-permute-done = f32[8,128,128]{2,1,0:T(8,128)S(1)} collective-permute-done((f32[8,128,128]{2,1,0:T(8,128)S(1)}, f32[8,128,128]{2,1,0:T(8,128)S(1)}, u32[]{:S(2)}, u32[]{:S(2)}) %collective-permute-start) | collective-permute-done | bytes 524320 | tf_op jit(solution)/shard_map/while/body/eval_jaxpr/ppermute | solution.py:15
  215.7 15.9 %collective-permute-done = f32[8,128,128]{2,1,0:T(8,128)S(1)} collective-permute-done((f32[8,128,128]{2,1,0:T(8,128)S(1)}, f32[8,128,128]{2,1,0:T(8,128)S(1)}, u32[]{:S(2)}, u32[]{:S(2)}) %collective-permute-start) | collective-permute-done | bytes 524320 | tf_op jit(solution)/shard_map/while/body/eval_jaxpr/ppermute | solution.py:15
  233.6 17.0 %collective-permute-done = f32[8,128,128]{2,1,0:T(8,128)S(1)} collective-permute-done((f32[8,128,128]{2,1,0:T(8,128)S(1)}, f32[8,128,128]{2,1,0:T(8,128)S(1)}, u32[]{:S(2)}, u32[]{:S(2)}) %collective-permute-start) | collective-permute-done | bytes 524320 | tf_op jit(solution)/shard_map/while/body/eval_jaxpr/ppermute | solution.py:15
  252.7 18.0 %collective-permute-done = f32[8,128,128]{2,1,0:T(8,128)S(1)} collective-permute-done((f32[8,128,128]{2,1,0:T(8,128)S(1)}, f32[8,128,128]{2,1,0:T(8,128)S(1)}, u32[]{:S(2)}, u32[]{:S(2)}) %collective-permute-start) | collective-permute-done | bytes 524320 | tf_op jit(solution)/shard_map/while/body/eval_jaxpr/ppermute | solution.py:15
  272.7 17.1 %collective-permute-done = f32[8,128,128]{2,1,0:T(8,128)S(1)} collective-permute-done((f32[8,128,128]{2,1,0:T(8,128)S(1)}, f32[8,128,128]{2,1,0:T(8,128)S(1)}, u32[]{:S(2)}, u32[]{:S(2)}) %collective-permute-start) | collective-permute-done | bytes 524320 | tf_op jit(solution)/shard_map/while/body/eval_jaxpr/ppermute | solution.py:15
  291.9 16.3 %collective-permute-done = f32[8,128,128]{2,1,0:T(8,128)S(1)} collective-permute-done((f32[8,128,128]{2,1,0:T(8,128)S(1)}, f32[8,128,128]{2,1,0:T(8,128)S(1)}, u32[]{:S(2)}, u32[]{:S(2)}) %collective-permute-start) | collective-permute-done | bytes 524320 | tf_op jit(solution)/shard_map/while/body/eval_jaxpr/ppermute | solution.py:15
  310.2 15.4 %collective-permute-done = f32[8,128,128]{2,1,0:T(8,128)S(1)} collective-permute-done((f32[8,128,128]{2,1,0:T(8,128)S(1)}, f32[8,128,128]{2,1,0:T(8,128)S(1)}, u32[]{:S(2)}, u32[]{:S(2)}) %collective-permute-start) | collective-permute-done | bytes 524320 | tf_op jit(solution)/shard_map/while/body/eval_jaxpr/ppermute | solution.py:15
  327.7 14.4 %collective-permute-done = f32[8,128,128]{2,1,0:T(8,128)S(1)} collective-permute-done((f32[8,128,128]{2,1,0:T(8,128)S(1)}, f32[8,128,128]{2,1,0:T(8,128)S(1)}, u32[]{:S(2)}, u32[]{:S(2)}) %collective-permute-start) | collective-permute-done | bytes 524320 | tf_op jit(solution)/shard_map/while/body/eval_jaxpr/ppermute | solution.py:15
  344.2 13.5 %collective-permute-done = f32[8,128,128]{2,1,0:T(8,128)S(1)} collective-permute-done((f32[8,128,128]{2,1,0:T(8,128)S(1)}, f32[8,128,128]{2,1,0:T(8,128)S(1)}, u32[]{:S(2)}, u32[]{:S(2)}) %collective-permute-start) | collective-permute-done | bytes 524320 | tf_op jit(solution)/shard_map/while/body/eval_jaxpr/ppermute | solution.py:15
  359.7 12.6 %collective-permute-done = f32[8,128,128]{2,1,0:T(8,128)S(1)} collective-permute-done((f32[8,128,128]{2,1,0:T(8,128)S(1)}, f32[8,128,128]{2,1,0:T(8,128)S(1)}, u32[]{:S(2)}, u32[]{:S(2)}) %collective-permute-start) | collective-permute-done | bytes 524320 | tf_op jit(solution)/shard_map/while/body/eval_jaxpr/ppermute | solution.py:15
  388.9 12.5 %collective-permute-done = f32[8,128,128]{2,1,0:T(8,128)S(1)} collective-permute-done((f32[8,128,128]{2,1,0:T(8,128)S(1)}, f32[8,128,128]{2,1,0:T(8,128)S(1)}, u32[]{:S(2)}, u32[]{:S(2)}) %collective-permute-start) | collective-permute-done | bytes 524320 | tf_op jit(solution)/shard_map/while/body/eval_jaxpr/ppermute | solution.py:15
  403.4 13.3 %collective-permute-done = f32[8,128,128]{2,1,0:T(8,128)S(1)} collective-permute-done((f32[8,128,128]{2,1,0:T(8,128)S(1)}, f32[8,128,128]{2,1,0:T(8,128)S(1)}, u32[]{:S(2)}, u32[]{:S(2)}) %collective-permute-start) | collective-permute-done | bytes 524320 | tf_op jit(solution)/shard_map/while/body/eval_jaxpr/ppermute | solution.py:15
  418.8 14.4 %collective-permute-done = f32[8,128,128]{2,1,0:T(8,128)S(1)} collective-permute-done((f32[8,128,128]{2,1,0:T(8,128)S(1)}, f32[8,128,128]{2,1,0:T(8,128)S(1)}, u32[]{:S(2)}, u32[]{:S(2)}) %collective-permute-start) | collective-permute-done | bytes 524320 | tf_op jit(solution)/shard_map/while/body/eval_jaxpr/ppermute | solution.py:15
  435.3 15.5 %collective-permute-done = f32[8,128,128]{2,1,0:T(8,128)S(1)} collective-permute-done((f32[8,128,128]{2,1,0:T(8,128)S(1)}, f32[8,128,128]{2,1,0:T(8,128)S(1)}, u32[]{:S(2)}, u32[]{:S(2)}) %collective-permute-start) | collective-permute-done | bytes 524320 | tf_op jit(solution)/shard_map/while/body/eval_jaxpr/ppermute | solution.py:15
  452.9 16.6 %collective-permute-done = f32[8,128,128]{2,1,0:T(8,128)S(1)} collective-permute-done((f32[8,128,128]{2,1,0:T(8,128)S(1)}, f32[8,128,128]{2,1,0:T(8,128)S(1)}, u32[]{:S(2)}, u32[]{:S(2)}) %collective-permute-start) | collective-permute-done | bytes 524320 | tf_op jit(solution)/shard_map/while/body/eval_jaxpr/ppermute | solution.py:15
  471.5 17.7 %collective-permute-done = f32[8,128,128]{2,1,0:T(8,128)S(1)} collective-permute-done((f32[8,128,128]{2,1,0:T(8,128)S(1)}, f32[8,128,128]{2,1,0:T(8,128)S(1)}, u32[]{:S(2)}, u32[]{:S(2)}) %collective-permute-start) | collective-permute-done | bytes 524320 | tf_op jit(solution)/shard_map/while/body/eval_jaxpr/ppermute | solution.py:15
  491.3 17.3 %collective-permute-done = f32[8,128,128]{2,1,0:T(8,128)S(1)} collective-permute-done((f32[8,128,128]{2,1,0:T(8,128)S(1)}, f32[8,128,128]{2,1,0:T(8,128)S(1)}, u32[]{:S(2)}, u32[]{:S(2)}) %collective-permute-start) | collective-permute-done | bytes 524320 | tf_op jit(solution)/shard_map/while/body/eval_jaxpr/ppermute | solution.py:15
  510.6 16.4 %collective-permute-done = f32[8,128,128]{2,1,0:T(8,128)S(1)} collective-permute-done((f32[8,128,128]{2,1,0:T(8,128)S(1)}, f32[8,128,128]{2,1,0:T(8,128)S(1)}, u32[]{:S(2)}, u32[]{:S(2)}) %collective-permute-start) | collective-permute-done | bytes 524320 | tf_op jit(solution)/shard_map/while/body/eval_jaxpr/ppermute | solution.py:15
  529.1 15.5 %collective-permute-done = f32[8,128,128]{2,1,0:T(8,128)S(1)} collective-permute-done((f32[8,128,128]{2,1,0:T(8,128)S(1)}, f32[8,128,128]{2,1,0:T(8,128)S(1)}, u32[]{:S(2)}, u32[]{:S(2)}) %collective-permute-start) | collective-permute-done | bytes 524320 | tf_op jit(solution)/shard_map/while/body/eval_jaxpr/ppermute | solution.py:15
  546.7 12.5 %collective-permute-done = f32[8,128,128]{2,1,0:T(8,128)S(1)} collective-permute-done((f32[8,128,128]{2,1,0:T(8,128)S(1)}, f32[8,128,128]{2,1,0:T(8,128)S(1)}, u32[]{:S(2)}, u32[]{:S(2)}) %collective-permute-start) | collective-permute-done | bytes 524320 | tf_op jit(solution)/shard_map/while/body/eval_jaxpr/ppermute | solution.py:15
  561.2 12.5 %collective-permute-done = f32[8,128,128]{2,1,0:T(8,128)S(1)} collective-permute-done((f32[8,128,128]{2,1,0:T(8,128)S(1)}, f32[8,128,128]{2,1,0:T(8,128)S(1)}, u32[]{:S(2)}, u32[]{:S(2)}) %collective-permute-start) | collective-permute-done | bytes 524320 | tf_op jit(solution)/shard_map/while/body/eval_jaxpr/ppermute | solution.py:15
  584.3 31.8 %all_to_all.16 = bf16[8,128,1024]{2,1,0:T(8,128)(2,1)S(1)} all-to-all(bf16[8,128,1024]{2,1,0:T(8,128)(2,1)} %convert_element_type.20), channel_id=1, replica_groups=mesh['seq'=32,'head'=8] {'head'}, dimensions={0} | all-to-all | bytes 4194304 | tf_op jit(solution)/shard_map/all_to_all | solution.py:84
  (106 shorter events, 145.4 us)
Async XLA Ops:
  33.8 12.1 %copy-start.1 = (bf16[512,1024]{0,1:T(8,128)(2,1)S(1)}, bf16[512,1024]{0,1:T(8,128)(2,1)}, u32[]{:S(2)}) copy-start(bf16[512,1024]{0,1:T(8,128)(2,1)} %copy.119) | copy-start | bytes 3145732
  51.4 18.9 %collective-permute-start = (f32[8,128,128]{2,1,0:T(8,128)S(1)}, f32[8,128,128]{2,1,0:T(8,128)S(1)}, u32[]{:S(2)}, u32[]{:S(2)}) collective-permute-start(f32[8,128,128]{2,1,0:T(8,128)S(1)} %multiply_add_fusion.2), channel_id=1, source_target_pairs={{0,8},{8,16},{16,24},{24,32},{32,40},{40,48},{48,56},{56,64},{64,7... | collective-permute-start | bytes 1572872 | tf_op jit(solution)/shard_map/while/body/eval_jaxpr/ppermute | solution.py:15
  70.4 18.0 %collective-permute-start = (f32[8,128,128]{2,1,0:T(8,128)S(1)}, f32[8,128,128]{2,1,0:T(8,128)S(1)}, u32[]{:S(2)}, u32[]{:S(2)}) collective-permute-start(f32[8,128,128]{2,1,0:T(8,128)S(1)} %multiply_add_fusion.2), channel_id=1, source_target_pairs={{0,8},{8,16},{16,24},{24,32},{32,40},{40,48},{48,56},{56,64},{64,7... | collective-permute-start | bytes 1572872 | tf_op jit(solution)/shard_map/while/body/eval_jaxpr/ppermute | solution.py:15
  88.5 17.1 %collective-permute-start = (f32[8,128,128]{2,1,0:T(8,128)S(1)}, f32[8,128,128]{2,1,0:T(8,128)S(1)}, u32[]{:S(2)}, u32[]{:S(2)}) collective-permute-start(f32[8,128,128]{2,1,0:T(8,128)S(1)} %multiply_add_fusion.2), channel_id=1, source_target_pairs={{0,8},{8,16},{16,24},{24,32},{32,40},{40,48},{48,56},{56,64},{64,7... | collective-permute-start | bytes 1572872 | tf_op jit(solution)/shard_map/while/body/eval_jaxpr/ppermute | solution.py:15
  105.7 16.2 %collective-permute-start = (f32[8,128,128]{2,1,0:T(8,128)S(1)}, f32[8,128,128]{2,1,0:T(8,128)S(1)}, u32[]{:S(2)}, u32[]{:S(2)}) collective-permute-start(f32[8,128,128]{2,1,0:T(8,128)S(1)} %multiply_add_fusion.2), channel_id=1, source_target_pairs={{0,8},{8,16},{16,24},{24,32},{32,40},{40,48},{48,56},{56,64},{64,7... | collective-permute-start | bytes 1572872 | tf_op jit(solution)/shard_map/while/body/eval_jaxpr/ppermute | solution.py:15
  122.0 15.2 %collective-permute-start = (f32[8,128,128]{2,1,0:T(8,128)S(1)}, f32[8,128,128]{2,1,0:T(8,128)S(1)}, u32[]{:S(2)}, u32[]{:S(2)}) collective-permute-start(f32[8,128,128]{2,1,0:T(8,128)S(1)} %multiply_add_fusion.2), channel_id=1, source_target_pairs={{0,8},{8,16},{16,24},{24,32},{32,40},{40,48},{48,56},{56,64},{64,7... | collective-permute-start | bytes 1572872 | tf_op jit(solution)/shard_map/while/body/eval_jaxpr/ppermute | solution.py:15
  137.4 14.4 %collective-permute-start = (f32[8,128,128]{2,1,0:T(8,128)S(1)}, f32[8,128,128]{2,1,0:T(8,128)S(1)}, u32[]{:S(2)}, u32[]{:S(2)}) collective-permute-start(f32[8,128,128]{2,1,0:T(8,128)S(1)} %multiply_add_fusion.2), channel_id=1, source_target_pairs={{0,8},{8,16},{16,24},{24,32},{32,40},{40,48},{48,56},{56,64},{64,7... | collective-permute-start | bytes 1572872 | tf_op jit(solution)/shard_map/while/body/eval_jaxpr/ppermute | solution.py:15
  151.9 14.4 %collective-permute-start = (f32[8,128,128]{2,1,0:T(8,128)S(1)}, f32[8,128,128]{2,1,0:T(8,128)S(1)}, u32[]{:S(2)}, u32[]{:S(2)}) collective-permute-start(f32[8,128,128]{2,1,0:T(8,128)S(1)} %multiply_add_fusion.2), channel_id=1, source_target_pairs={{0,8},{8,16},{16,24},{24,32},{32,40},{40,48},{48,56},{56,64},{64,7... | collective-permute-start | bytes 1572872 | tf_op jit(solution)/shard_map/while/body/eval_jaxpr/ppermute | solution.py:15
  166.4 14.6 %collective-permute-start = (f32[8,128,128]{2,1,0:T(8,128)S(1)}, f32[8,128,128]{2,1,0:T(8,128)S(1)}, u32[]{:S(2)}, u32[]{:S(2)}) collective-permute-start(f32[8,128,128]{2,1,0:T(8,128)S(1)} %multiply_add_fusion.2), channel_id=1, source_target_pairs={{0,8},{8,16},{16,24},{24,32},{32,40},{40,48},{48,56},{56,64},{64,7... | collective-permute-start | bytes 1572872 | tf_op jit(solution)/shard_map/while/body/eval_jaxpr/ppermute | solution.py:15
  181.1 15.7 %collective-permute-start = (f32[8,128,128]{2,1,0:T(8,128)S(1)}, f32[8,128,128]{2,1,0:T(8,128)S(1)}, u32[]{:S(2)}, u32[]{:S(2)}) collective-permute-start(f32[8,128,128]{2,1,0:T(8,128)S(1)} %multiply_add_fusion.2), channel_id=1, source_target_pairs={{0,8},{8,16},{16,24},{24,32},{32,40},{40,48},{48,56},{56,64},{64,7... | collective-permute-start | bytes 1572872 | tf_op jit(solution)/shard_map/while/body/eval_jaxpr/ppermute | solution.py:15
  196.9 16.7 %collective-permute-start = (f32[8,128,128]{2,1,0:T(8,128)S(1)}, f32[8,128,128]{2,1,0:T(8,128)S(1)}, u32[]{:S(2)}, u32[]{:S(2)}) collective-permute-start(f32[8,128,128]{2,1,0:T(8,128)S(1)} %multiply_add_fusion.2), channel_id=1, source_target_pairs={{0,8},{8,16},{16,24},{24,32},{32,40},{40,48},{48,56},{56,64},{64,7... | collective-permute-start | bytes 1572872 | tf_op jit(solution)/shard_map/while/body/eval_jaxpr/ppermute | solution.py:15
  213.7 17.8 %collective-permute-start = (f32[8,128,128]{2,1,0:T(8,128)S(1)}, f32[8,128,128]{2,1,0:T(8,128)S(1)}, u32[]{:S(2)}, u32[]{:S(2)}) collective-permute-start(f32[8,128,128]{2,1,0:T(8,128)S(1)} %multiply_add_fusion.2), channel_id=1, source_target_pairs={{0,8},{8,16},{16,24},{24,32},{32,40},{40,48},{48,56},{56,64},{64,7... | collective-permute-start | bytes 1572872 | tf_op jit(solution)/shard_map/while/body/eval_jaxpr/ppermute | solution.py:15
  231.7 19.0 %collective-permute-start = (f32[8,128,128]{2,1,0:T(8,128)S(1)}, f32[8,128,128]{2,1,0:T(8,128)S(1)}, u32[]{:S(2)}, u32[]{:S(2)}) collective-permute-start(f32[8,128,128]{2,1,0:T(8,128)S(1)} %multiply_add_fusion.2), channel_id=1, source_target_pairs={{0,8},{8,16},{16,24},{24,32},{32,40},{40,48},{48,56},{56,64},{64,7... | collective-permute-start | bytes 1572872 | tf_op jit(solution)/shard_map/while/body/eval_jaxpr/ppermute | solution.py:15
  250.7 19.9 %collective-permute-start = (f32[8,128,128]{2,1,0:T(8,128)S(1)}, f32[8,128,128]{2,1,0:T(8,128)S(1)}, u32[]{:S(2)}, u32[]{:S(2)}) collective-permute-start(f32[8,128,128]{2,1,0:T(8,128)S(1)} %multiply_add_fusion.2), channel_id=1, source_target_pairs={{0,8},{8,16},{16,24},{24,32},{32,40},{40,48},{48,56},{56,64},{64,7... | collective-permute-start | bytes 1572872 | tf_op jit(solution)/shard_map/while/body/eval_jaxpr/ppermute | solution.py:15
  270.8 19.1 %collective-permute-start = (f32[8,128,128]{2,1,0:T(8,128)S(1)}, f32[8,128,128]{2,1,0:T(8,128)S(1)}, u32[]{:S(2)}, u32[]{:S(2)}) collective-permute-start(f32[8,128,128]{2,1,0:T(8,128)S(1)} %multiply_add_fusion.2), channel_id=1, source_target_pairs={{0,8},{8,16},{16,24},{24,32},{32,40},{40,48},{48,56},{56,64},{64,7... | collective-permute-start | bytes 1572872 | tf_op jit(solution)/shard_map/while/body/eval_jaxpr/ppermute | solution.py:15
  290.0 18.2 %collective-permute-start = (f32[8,128,128]{2,1,0:T(8,128)S(1)}, f32[8,128,128]{2,1,0:T(8,128)S(1)}, u32[]{:S(2)}, u32[]{:S(2)}) collective-permute-start(f32[8,128,128]{2,1,0:T(8,128)S(1)} %multiply_add_fusion.2), channel_id=1, source_target_pairs={{0,8},{8,16},{16,24},{24,32},{32,40},{40,48},{48,56},{56,64},{64,7... | collective-permute-start | bytes 1572872 | tf_op jit(solution)/shard_map/while/body/eval_jaxpr/ppermute | solution.py:15
  308.3 17.3 %collective-permute-start = (f32[8,128,128]{2,1,0:T(8,128)S(1)}, f32[8,128,128]{2,1,0:T(8,128)S(1)}, u32[]{:S(2)}, u32[]{:S(2)}) collective-permute-start(f32[8,128,128]{2,1,0:T(8,128)S(1)} %multiply_add_fusion.2), channel_id=1, source_target_pairs={{0,8},{8,16},{16,24},{24,32},{32,40},{40,48},{48,56},{56,64},{64,7... | collective-permute-start | bytes 1572872 | tf_op jit(solution)/shard_map/while/body/eval_jaxpr/ppermute | solution.py:15
  325.7 16.4 %collective-permute-start = (f32[8,128,128]{2,1,0:T(8,128)S(1)}, f32[8,128,128]{2,1,0:T(8,128)S(1)}, u32[]{:S(2)}, u32[]{:S(2)}) collective-permute-start(f32[8,128,128]{2,1,0:T(8,128)S(1)} %multiply_add_fusion.2), channel_id=1, source_target_pairs={{0,8},{8,16},{16,24},{24,32},{32,40},{40,48},{48,56},{56,64},{64,7... | collective-permute-start | bytes 1572872 | tf_op jit(solution)/shard_map/while/body/eval_jaxpr/ppermute | solution.py:15
  342.2 15.5 %collective-permute-start = (f32[8,128,128]{2,1,0:T(8,128)S(1)}, f32[8,128,128]{2,1,0:T(8,128)S(1)}, u32[]{:S(2)}, u32[]{:S(2)}) collective-permute-start(f32[8,128,128]{2,1,0:T(8,128)S(1)} %multiply_add_fusion.2), channel_id=1, source_target_pairs={{0,8},{8,16},{16,24},{24,32},{32,40},{40,48},{48,56},{56,64},{64,7... | collective-permute-start | bytes 1572872 | tf_op jit(solution)/shard_map/while/body/eval_jaxpr/ppermute | solution.py:15
  357.8 14.5 %collective-permute-start = (f32[8,128,128]{2,1,0:T(8,128)S(1)}, f32[8,128,128]{2,1,0:T(8,128)S(1)}, u32[]{:S(2)}, u32[]{:S(2)}) collective-permute-start(f32[8,128,128]{2,1,0:T(8,128)S(1)} %multiply_add_fusion.2), channel_id=1, source_target_pairs={{0,8},{8,16},{16,24},{24,32},{32,40},{40,48},{48,56},{56,64},{64,7... | collective-permute-start | bytes 1572872 | tf_op jit(solution)/shard_map/while/body/eval_jaxpr/ppermute | solution.py:15
  372.5 14.4 %collective-permute-start = (f32[8,128,128]{2,1,0:T(8,128)S(1)}, f32[8,128,128]{2,1,0:T(8,128)S(1)}, u32[]{:S(2)}, u32[]{:S(2)}) collective-permute-start(f32[8,128,128]{2,1,0:T(8,128)S(1)} %multiply_add_fusion.2), channel_id=1, source_target_pairs={{0,8},{8,16},{16,24},{24,32},{32,40},{40,48},{48,56},{56,64},{64,7... | collective-permute-start | bytes 1572872 | tf_op jit(solution)/shard_map/while/body/eval_jaxpr/ppermute | solution.py:15
  387.0 14.4 %collective-permute-start = (f32[8,128,128]{2,1,0:T(8,128)S(1)}, f32[8,128,128]{2,1,0:T(8,128)S(1)}, u32[]{:S(2)}, u32[]{:S(2)}) collective-permute-start(f32[8,128,128]{2,1,0:T(8,128)S(1)} %multiply_add_fusion.2), channel_id=1, source_target_pairs={{0,8},{8,16},{16,24},{24,32},{32,40},{40,48},{48,56},{56,64},{64,7... | collective-permute-start | bytes 1572872 | tf_op jit(solution)/shard_map/while/body/eval_jaxpr/ppermute | solution.py:15
  401.5 15.3 %collective-permute-start = (f32[8,128,128]{2,1,0:T(8,128)S(1)}, f32[8,128,128]{2,1,0:T(8,128)S(1)}, u32[]{:S(2)}, u32[]{:S(2)}) collective-permute-start(f32[8,128,128]{2,1,0:T(8,128)S(1)} %multiply_add_fusion.2), channel_id=1, source_target_pairs={{0,8},{8,16},{16,24},{24,32},{32,40},{40,48},{48,56},{56,64},{64,7... | collective-permute-start | bytes 1572872 | tf_op jit(solution)/shard_map/while/body/eval_jaxpr/ppermute | solution.py:15
  416.9 16.4 %collective-permute-start = (f32[8,128,128]{2,1,0:T(8,128)S(1)}, f32[8,128,128]{2,1,0:T(8,128)S(1)}, u32[]{:S(2)}, u32[]{:S(2)}) collective-permute-start(f32[8,128,128]{2,1,0:T(8,128)S(1)} %multiply_add_fusion.2), channel_id=1, source_target_pairs={{0,8},{8,16},{16,24},{24,32},{32,40},{40,48},{48,56},{56,64},{64,7... | collective-permute-start | bytes 1572872 | tf_op jit(solution)/shard_map/while/body/eval_jaxpr/ppermute | solution.py:15
  433.4 17.4 %collective-permute-start = (f32[8,128,128]{2,1,0:T(8,128)S(1)}, f32[8,128,128]{2,1,0:T(8,128)S(1)}, u32[]{:S(2)}, u32[]{:S(2)}) collective-permute-start(f32[8,128,128]{2,1,0:T(8,128)S(1)} %multiply_add_fusion.2), channel_id=1, source_target_pairs={{0,8},{8,16},{16,24},{24,32},{32,40},{40,48},{48,56},{56,64},{64,7... | collective-permute-start | bytes 1572872 | tf_op jit(solution)/shard_map/while/body/eval_jaxpr/ppermute | solution.py:15
  450.9 18.5 %collective-permute-start = (f32[8,128,128]{2,1,0:T(8,128)S(1)}, f32[8,128,128]{2,1,0:T(8,128)S(1)}, u32[]{:S(2)}, u32[]{:S(2)}) collective-permute-start(f32[8,128,128]{2,1,0:T(8,128)S(1)} %multiply_add_fusion.2), channel_id=1, source_target_pairs={{0,8},{8,16},{16,24},{24,32},{32,40},{40,48},{48,56},{56,64},{64,7... | collective-permute-start | bytes 1572872 | tf_op jit(solution)/shard_map/while/body/eval_jaxpr/ppermute | solution.py:15
  469.6 19.7 %collective-permute-start = (f32[8,128,128]{2,1,0:T(8,128)S(1)}, f32[8,128,128]{2,1,0:T(8,128)S(1)}, u32[]{:S(2)}, u32[]{:S(2)}) collective-permute-start(f32[8,128,128]{2,1,0:T(8,128)S(1)} %multiply_add_fusion.2), channel_id=1, source_target_pairs={{0,8},{8,16},{16,24},{24,32},{32,40},{40,48},{48,56},{56,64},{64,7... | collective-permute-start | bytes 1572872 | tf_op jit(solution)/shard_map/while/body/eval_jaxpr/ppermute | solution.py:15
  489.4 19.2 %collective-permute-start = (f32[8,128,128]{2,1,0:T(8,128)S(1)}, f32[8,128,128]{2,1,0:T(8,128)S(1)}, u32[]{:S(2)}, u32[]{:S(2)}) collective-permute-start(f32[8,128,128]{2,1,0:T(8,128)S(1)} %multiply_add_fusion.2), channel_id=1, source_target_pairs={{0,8},{8,16},{16,24},{24,32},{32,40},{40,48},{48,56},{56,64},{64,7... | collective-permute-start | bytes 1572872 | tf_op jit(solution)/shard_map/while/body/eval_jaxpr/ppermute | solution.py:15
  508.7 18.4 %collective-permute-start = (f32[8,128,128]{2,1,0:T(8,128)S(1)}, f32[8,128,128]{2,1,0:T(8,128)S(1)}, u32[]{:S(2)}, u32[]{:S(2)}) collective-permute-start(f32[8,128,128]{2,1,0:T(8,128)S(1)} %multiply_add_fusion.2), channel_id=1, source_target_pairs={{0,8},{8,16},{16,24},{24,32},{32,40},{40,48},{48,56},{56,64},{64,7... | collective-permute-start | bytes 1572872 | tf_op jit(solution)/shard_map/while/body/eval_jaxpr/ppermute | solution.py:15
  527.2 17.4 %collective-permute-start = (f32[8,128,128]{2,1,0:T(8,128)S(1)}, f32[8,128,128]{2,1,0:T(8,128)S(1)}, u32[]{:S(2)}, u32[]{:S(2)}) collective-permute-start(f32[8,128,128]{2,1,0:T(8,128)S(1)} %multiply_add_fusion.2), channel_id=1, source_target_pairs={{0,8},{8,16},{16,24},{24,32},{32,40},{40,48},{48,56},{56,64},{64,7... | collective-permute-start | bytes 1572872 | tf_op jit(solution)/shard_map/while/body/eval_jaxpr/ppermute | solution.py:15
  544.7 14.4 %collective-permute-start = (f32[8,128,128]{2,1,0:T(8,128)S(1)}, f32[8,128,128]{2,1,0:T(8,128)S(1)}, u32[]{:S(2)}, u32[]{:S(2)}) collective-permute-start(f32[8,128,128]{2,1,0:T(8,128)S(1)} %multiply_add_fusion.2), channel_id=1, source_target_pairs={{0,8},{8,16},{16,24},{24,32},{32,40},{40,48},{48,56},{56,64},{64,7... | collective-permute-start | bytes 1572872 | tf_op jit(solution)/shard_map/while/body/eval_jaxpr/ppermute | solution.py:15
  559.3 14.4 %collective-permute-start = (f32[8,128,128]{2,1,0:T(8,128)S(1)}, f32[8,128,128]{2,1,0:T(8,128)S(1)}, u32[]{:S(2)}, u32[]{:S(2)}) collective-permute-start(f32[8,128,128]{2,1,0:T(8,128)S(1)} %multiply_add_fusion.2), channel_id=1, source_target_pairs={{0,8},{8,16},{16,24},{24,32},{32,40},{40,48},{48,56},{56,64},{64,7... | collective-permute-start | bytes 1572872 | tf_op jit(solution)/shard_map/while/body/eval_jaxpr/ppermute | solution.py:15
  (4 other events, 17.9 us)
where the time goes:
time: 624 us; the launch traced here: 623 us
  waiting for transfers between devices  457 us (73%)
  starting transfers between devices  61.1 us (10%)
  matrix products  36.8 us (6%)
  blocking collectives  31.8 us (5%)
  local copies, waits for them, and re-layouts  27 us (4%)
  other arithmetic  8.04 us (1%)
    ppermute x31, waiting for transfers between devices, from_behind(): return lax.ppermute(block, axis, route)  457 us
    ppermute x31, starting transfers between devices, from_behind(): return lax.ppermute(block, axis, route)  61.1 us
    all_to_all x1, blocking collectives, on_device(): lax.all_to_all(head_rows, 'head', split_axis=0, concat_axis=1, tiled=True)  31.8 us
    dot_general x2, matrix products, on_device(): jnp.einsum('hts,shd->thd', weights, value_heads[:last_row], precision=THR...  17.4 us
  transfers between devices with their start and end apart: 31, of which 31 were waited for; matrix products, arithmetic and copies ran while one was open for 0% of the time, Pallas kernels for 0%

commit v1 on v0

v1 whole, which is shorter than its diff:
```python
import functools

import jax
import jax.numpy as jnp
from jax import lax
from jax.experimental import pallas as pl
from jax.experimental.pallas import tpu as pltpu
from jax.sharding import PartitionSpec as P

HD = 128
CHUNK = 128
MESH = pl.DeviceIdType.MESH
F32 = jnp.float32
BF16 = jnp.bfloat16
RING_Y = 4


def exact_dot(a, b):
    return jnp.dot(a, b, precision=lax.Precision.HIGHEST, preferred_element_type=F32)


def two_terms(x):
    high = x.astype(BF16)
    low = (x - high.astype(F32)).astype(BF16)
    return high, low


def wait_for(ref, sem):
    pltpu.make_async_copy(ref, ref, sem).wait()


def kernel(
    sizes,
    q_hbm, k_hbm, v_hbm, decay_hbm, gain_ref, out_hbm,
    q, k, v, decay, grow, fade, chunk_fade, start_fade, shrink,
    state, starts, inner, y_got, z_own, z_got, back, incoming, normed,
    end_y, end_z_own, end_z,
    decay_sem, q_sem, k_sem, v_sem,
    end_send, end_y_recv, end_z_recv, y_send, y_recv, z_send, z_recv, b_send, b_recv, x_send, x_recv, own_sem,
):
    heads, chunks, ny, nz = sizes
    piece = HD // ny
    seq = lax.axis_index("seq")
    head_at = lax.axis_index("head")
    my_z, my_y = seq // ny, lax.rem(seq, ny)

    def y_peer(i):
        other = lax.rem(my_y + i, ny)
        return other, {"seq": my_z * ny + other}

    def z_peer(i):
        other = lax.rem(my_z + i, nz)
        return other, {"seq": other * ny + my_y}

    def x_peer(i):
        other = lax.rem(head_at + i, chunks)
        return other, {"head": other}

    def remote(src, dst, send, recv, device):
        return pltpu.make_async_remote_copy(src, dst, send, recv, device_id=device, device_id_type=MESH)

    def columns(h):
        return pl.ds(pl.multiple_of(h * HD, HD), HD)

    def load(array_hbm, array, sems, h):
        return pltpu.make_async_copy(array_hbm.at[:, columns(h)], array.at[h], sems.at[h])

    decay_copy = pltpu.make_async_copy(decay_hbm, decay, decay_sem)
    decay_copy.start()
    barrier = pltpu.get_barrier_semaphore()
    for i in range(1, ny):
        pl.semaphore_signal(barrier, inc=1, device_id=y_peer(i)[1], device_id_type=MESH)
    for i in range(1, nz):
        pl.semaphore_signal(barrier, inc=1, device_id=z_peer(i)[1], device_id_type=MESH)
    for i in range(1, chunks):
        pl.semaphore_signal(barrier, inc=1, device_id=x_peer(i)[1], device_id_type=MESH)

    @pl.loop(0, heads)
    def _(h):
        load(k_hbm, k, k_sem, h).start()
        load(v_hbm, v, v_sem, h).start()

    @pl.loop(0, heads)
    def _(h):
        load(q_hbm, q, q_sem, h).start()

    decay_copy.wait()
    row = lax.broadcasted_iota(jnp.int32, (CHUNK, CHUNK), 0)
    col = lax.broadcasted_iota(jnp.int32, (CHUNK, CHUNK), 1)
    rates = jnp.concatenate([decay[j * CHUNK : (j + 1) * CHUNK, :].T for j in range(chunks)], axis=0)
    cumulative = exact_dot(rates, (row <= col).astype(F32))
    ending = exact_dot(rates, jnp.ones((CHUNK, CHUNK), F32))
    grow[...] = jnp.exp(cumulative)
    fade[...] = jnp.exp(cumulative - ending)
    chunk_fade[...] = jnp.exp(-ending)
    so_far = jnp.zeros((heads, HD), F32)
    for j in range(chunks):
        start_fade[j * heads : (j + 1) * heads, :] = jnp.exp(-so_far)
        so_far = so_far + ending[j * heads : (j + 1) * heads, :]
    end_y[my_y] = so_far
    shrink[...] = jnp.exp(-cumulative).T

    def local_state(h):
        load(k_hbm, k, k_sem, h).wait()
        load(v_hbm, v, v_sem, h).wait()
        total = jnp.zeros((HD, HD), F32)
        for j in range(chunks):
            rows = slice(j * CHUNK, (j + 1) * CHUNK)
            at = pl.ds(j * heads + h, 1)
            starts[h, j, 0:HD, :], starts[h, j, HD : 2 * HD, :] = two_terms(total)
            keys = k[h, rows, :].astype(F32).T * fade[at, :]
            values = v[h, rows, :]
            added = jnp.dot(
                jnp.concatenate(two_terms(keys), axis=1),
                jnp.concatenate([values, values], axis=0),
                preferred_element_type=F32,
            )
            total = total * chunk_fade[at, :] + added
        state[h] = total
        y_got[h, my_y] = state[h, pl.ds(pl.multiple_of(my_y * piece, piece), piece), :]

    def send_y(h):
        for i in range(1, ny):
            other, device = y_peer(i)
            rows = pl.ds(pl.multiple_of(other * piece, piece), piece)
            remote(state.at[h, rows], y_got.at[h, my_y], y_send, y_recv.at[h], device).start()

    def group_total(h):
        wait_for(y_got.at[h, pl.ds(0, ny - 1)], y_recv.at[h])
        total = y_got[h, 0]
        for y in range(1, ny):
            total = total * jnp.exp(-end_y[y, pl.ds(h, 1), :]) + y_got[h, y]
        z_own[h] = total
        z_got[h, my_z] = total
        for i in range(1, nz):
            device = z_peer(i)[1]
            remote(z_own.at[h], z_got.at[h, my_z], z_send, z_recv.at[h], device).start()

    def hand_back(h):
        wait_for(z_got.at[h, pl.ds(0, nz - 1)], z_recv.at[h])

        def add(z, total):
            return total * jnp.exp(-end_z[z, pl.ds(h, 1), :]) + z_got[h, z]

        total = lax.fori_loop(0, my_z, add, jnp.zeros((piece, HD), F32))
        for y in range(ny):
            back[h, y] = total
            if y + 1 < ny:
                total = total * jnp.exp(-end_y[y, pl.ds(h, 1), :]) + y_got[h, y]
        mine = pl.ds(pl.multiple_of(my_y * piece, piece), piece)
        incoming[h, mine, :] = back[h, my_y]
        for i in range(1, ny):
            other, device = y_peer(i)
            remote(back.at[h, other], incoming.at[h, mine], b_send, b_recv.at[h], device).start()

    def within(h):
        load(q_hbm, q, q_sem, h).wait()
        causal = row >= col
        for j in range(chunks):
            rows = slice(j * CHUNK, (j + 1) * CHUNK)
            at = pl.ds(j * heads + h, 1)
            queries, keys, values = q[h, rows, :], k[h, rows, :], v[h, rows, :]
            scores = lax.dot_general(queries, keys, (((1,), (1,)), ((), ())), preferred_element_type=F32)
            weights = jnp.where(causal, scores * grow[at, :], 0.0)
            inner[h, rows, :] = jnp.dot(
                jnp.concatenate(two_terms(weights), axis=1),
                jnp.concatenate([values, values], axis=0),
                preferred_element_type=F32,
            ) + jnp.dot(
                jnp.concatenate([queries, queries], axis=1), starts[h, j], preferred_element_type=F32
            )

    def finish(h):
        wait_for(incoming.at[h, pl.ds(0, (ny - 1) * piece)], b_recv.at[h])
        entering = jnp.concatenate(two_terms(incoming[h]), axis=0)
        gain = gain_ref[pl.ds(h, 1), :]
        target = pl.ds(pl.multiple_of((head_at * heads + h) * HD, HD), HD)
        lane = lax.broadcasted_iota(jnp.int32, (CHUNK, chunks * heads), 1)
        for i in range(1, chunks + 1):
            j, device = x_peer(i)
            rows = pl.ds(pl.multiple_of(j * CHUNK, CHUNK), CHUNK)
            at = j * heads + h
            queries = q[h, rows, :]
            carried = jnp.dot(
                jnp.concatenate([queries, queries], axis=1), entering, preferred_element_type=F32
            )
            scale = jnp.sum(jnp.where(lane == at, shrink[...], 0.0), axis=1, keepdims=True)
            raw = (inner[h, rows, :] + carried * start_fade[pl.ds(at, 1), :]) * scale
            square = jnp.mean(raw * raw, axis=1, keepdims=True)
            normed[h, j] = (raw * lax.rsqrt(square + 1e-06) * gain).astype(BF16)
            if i < chunks:
                remote(normed.at[h, j], out_hbm.at[:, target], x_send, x_recv, device).start()
            else:
                pltpu.make_async_copy(normed.at[h, j], out_hbm.at[:, target], own_sem.at[h]).start()

    local_state(0)
    pl.semaphore_wait(barrier, ny + nz + chunks - 3)
    for i in range(1, ny):
        remote(end_y.at[my_y], end_y.at[my_y], end_send, end_y_recv, y_peer(i)[1]).start()
    send_y(0)

    @pl.loop(1, heads)
    def _(h):
        local_state(h)
        send_y(h)

    wait_for(end_y.at[pl.ds(0, ny - 1)], end_y_recv)
    group_end = end_y[0]
    for y in range(1, ny):
        group_end = group_end + end_y[y]
    end_z_own[...] = group_end
    end_z[my_z] = group_end
    for i in range(1, nz):
        remote(end_z_own, end_z.at[my_z], end_send, end_z_recv, z_peer(i)[1]).start()

    @pl.loop(0, heads)
    def _(h):
        group_total(h)

    within(0)
    wait_for(end_z.at[pl.ds(0, nz - 1)], end_z_recv)
    hand_back(0)

    @pl.loop(1, heads)
    def _(h):
        within(h)
        hand_back(h)
        finish(h - 1)

    finish(heads - 1)

    wait_for(end_y.at[pl.ds(0, ny - 1)], end_send)
    wait_for(end_z.at[pl.ds(0, nz - 1)], end_send)

    @pl.loop(0, heads)
    def _(h):
        wait_for(y_got.at[h, pl.ds(0, ny - 1)], y_send)
        wait_for(z_got.at[h, pl.ds(0, nz - 1)], z_send)
        wait_for(back.at[h, pl.ds(0, ny - 1)], b_send)
        wait_for(normed.at[h, pl.ds(0, chunks - 1)], x_send)
        target = pl.ds(pl.multiple_of((head_at * heads + h) * HD, HD), HD)
        pltpu.make_async_copy(normed.at[h, head_at], out_hbm.at[:, target], own_sem.at[h]).wait()

    wait_for(out_hbm.at[:, pl.ds(0, (chunks - 1) * heads * HD)], x_recv)


def on_device(lin_query, lin_key, lin_value, log_decay, norm_gain):
    tokens, width = lin_query.shape
    heads, chunks = width // HD, tokens // CHUNK
    ny = RING_Y
    nz = lax.axis_size("seq") // ny
    piece = HD // ny
    rows = chunks * heads
    any_space = pl.BlockSpec(memory_space=pl.ANY)
    dma = pltpu.SemaphoreType.DMA
    return pl.pallas_call(
        functools.partial(kernel, (heads, chunks, ny, nz)),
        out_shape=jax.ShapeDtypeStruct((CHUNK, chunks * width), BF16),
        in_specs=[any_space] * 4 + [pl.BlockSpec(memory_space=pltpu.VMEM)],
        out_specs=any_space,
        scratch_shapes=[
            pltpu.VMEM((heads, tokens, HD), BF16),
            pltpu.VMEM((heads, tokens, HD), BF16),
            pltpu.VMEM((heads, tokens, HD), BF16),
            pltpu.VMEM((tokens, heads), F32),
            pltpu.VMEM((rows, CHUNK), F32),
            pltpu.VMEM((rows, CHUNK), F32),
            pltpu.VMEM((rows, CHUNK), F32),
            pltpu.VMEM((rows, CHUNK), F32),
            pltpu.VMEM((CHUNK, rows), F32),
            pltpu.VMEM((heads, HD, HD), F32),
            pltpu.VMEM((heads, chunks, 2 * HD, HD), BF16),
            pltpu.VMEM((heads, tokens, HD), F32),
            pltpu.VMEM((heads, ny, piece, HD), F32),
            pltpu.VMEM((heads, piece, HD), F32),
            pltpu.VMEM((heads, nz, piece, HD), F32),
            pltpu.VMEM((heads, ny, piece, HD), F32),
            pltpu.VMEM((heads, HD, HD), F32),
            pltpu.VMEM((heads, chunks, CHUNK, HD), BF16),
            pltpu.VMEM((ny, heads, HD), F32),
            pltpu.VMEM((heads, HD), F32),
            pltpu.VMEM((nz, heads, HD), F32),
            dma, dma((heads,)), dma((heads,)), dma((heads,)),
            dma, dma, dma, dma, dma((heads,)), dma, dma((heads,)), dma, dma((heads,)), dma, dma,
            dma((heads,)),
        ],
        compiler_params=pltpu.CompilerParams(
            collective_id=0, has_side_effects=True, vmem_limit_bytes=52 * 2**20
        ),
        name="lightning",
    )(lin_query, lin_key, lin_value, log_decay, norm_gain.reshape(heads, HD))


def solution(mesh):
    in_specs = (P("seq", "head"), P("seq", "head"), P("seq", "head"), P("seq", "head"), P("head"))
    out_specs = P(("seq", "head"), None)
    return jax.shard_map(
        on_device, mesh=mesh, in_specs=in_specs, out_specs=out_specs, check_vma=False
    )
```

time: 624 us -> 58.5 us (0.09)
  the two profiles are of different devices: /device:TPU:128 before, /device:TPU:1 now
where the time goes in v1:
time: 58.5 us; the launch traced here: 58.2 us
  Pallas kernels  53.5 us (91%)
  local copies, waits for them, and re-layouts  4.73 us (8%)
    pallas_call x1, Pallas kernels, on_device(): pl.pallas_call(functools.partial(kernel, (heads, chunks, ny, nz)), out_sh...  53.5 us
    unnamed x4, local copies, waits for them, and re-layouts  4.73 us

profile of v1, /device:TPU:1, one launch (start us, length us, event | category | flops | bytes accessed | tf_op | source)
XLA Modules:
  0.0 58.2 jit_solution(14656769798831555090)
XLA Ops:
  0.0 0.9 %copy.6.decay_hbm = f32[1024,8]{1,0:T(8,128)S(1)} copy(f32[1024,8]{0,1:T(8,128)} %param.8) | data formatting | bytes 65536 | tf_op args[3]
  1.0 0.0 copy-start
  1.0 0.7 %copy-done = f32[1024]{0:T(1024)S(1)} copy-done((f32[1024]{0:T(1024)S(1)}, f32[1024]{0:T(1024)}, u32[]{:S(2)}) %copy-start) | copy-done | bytes 4120
  1.7 53.5 %lightning.1 = bf16[128,8192]{1,0:T(8,128)(2,1)} custom-call(bf16[1024,1024]{1,0:T(8,128)(2,1)} %q_hbm.1, bf16[1024,1024]{1,0:T(8,128)(2,1)} %k_hbm.1, bf16[1024,1024]{1,0:T(8,128)(2,1)} %v_hbm.1, f32[1024,8]{1,0:T(8,128)S(1)} %copy.6.decay_hbm, f32[8,128]{1,0:T(8,128)S(1)} %bitcast.1), custom_call_target="tpu_custom_call" | custom-call | tf_op jit(solution)/shard_map/lightning/pallas_call | solution.py:256
  55.2 3.1 %copy.8 = bf16[128,8192]{1,0:T(8,128)(2,1)} copy(bf16[128,8192]{1,0:T(8,128)(2,1)} %lightning.1) | data formatting | bytes 4194304
Async XLA Ops:
  1.0 0.7 %copy-start = (f32[1024]{0:T(1024)S(1)}, f32[1024]{0:T(1024)}, u32[]{:S(2)}) copy-start(f32[1024]{0:T(1024)} %param.9) | copy-start | bytes 12292

commit v2 on v1

--- a/solution.py
+++ b/solution.py
@@ -13,6 +13,7 @@
 F32 = jnp.float32
 BF16 = jnp.bfloat16
 RING_Y = 4
+DIRECT = 4
 
 
 def exact_dot(a, b):
@@ -31,15 +32,18 @@
 
 def kernel(
     sizes,
-    q_hbm, k_hbm, v_hbm, decay_hbm, gain_ref, out_hbm,
-    q, k, v, decay, grow, fade, chunk_fade, start_fade, shrink,
+    q_hbm, k_hbm, v_hbm, decay_hbm, gain_hbm, out_hbm,
+    q, k, v, decay, gains, grow, fade, chunk_fade, start_fade, shrink,
     state, starts, inner, y_got, z_own, z_got, back, incoming, normed,
+    group, group_got, group_back, group_in,
     end_y, end_z_own, end_z,
-    decay_sem, q_sem, k_sem, v_sem,
+    decay_sem, gain_sem, q_sem, k_sem, v_sem,
     end_send, end_y_recv, end_z_recv, y_send, y_recv, z_send, z_recv, b_send, b_recv, x_send, x_recv, own_sem,
+    g_send, g_recv, gb_send, gb_recv,
 ):
     heads, chunks, ny, nz = sizes
     piece = HD // ny
+    share = (heads - DIRECT) * piece // nz
     seq = lax.axis_index("seq")
     head_at = lax.axis_index("head")
     my_z, my_y = seq // ny, lax.rem(seq, ny)
@@ -62,11 +66,16 @@
     def columns(h):
         return pl.ds(pl.multiple_of(h * HD, HD), HD)
 
-    def load(array_hbm, array, sems, h):
-        return pltpu.make_async_copy(array_hbm.at[:, columns(h)], array.at[h], sems.at[h])
-
     decay_copy = pltpu.make_async_copy(decay_hbm, decay, decay_sem)
     decay_copy.start()
+    gain_copy = pltpu.make_async_copy(gain_hbm, gains, gain_sem)
+    gain_copy.start()
+    k_copy = pltpu.make_async_copy(k_hbm, k, k_sem)
+    k_copy.start()
+    v_copy = pltpu.make_async_copy(v_hbm, v, v_sem)
+    v_copy.start()
+    q_copy = pltpu.make_async_copy(q_hbm, q, q_sem)
+    q_copy.start()
     barrier = pltpu.get_barrier_semaphore()
     for i in range(1, ny):
         pl.semaphore_signal(barrier, inc=1, device_id=y_peer(i)[1], device_id_type=MESH)
@@ -75,19 +84,10 @@
     for i in range(1, chunks):
         pl.semaphore_signal(barrier, inc=1, device_id=x_peer(i)[1], device_id_type=MESH)
 
-    @pl.loop(0, heads)
-    def _(h):
-        load(k_hbm, k, k_sem, h).start()
-        load(v_hbm, v, v_sem, h).start()
-
-    @pl.loop(0, heads)
-    def _(h):
-        load(q_hbm, q, q_sem, h).start()
-
     decay_copy.wait()
     row = lax.broadcasted_iota(jnp.int32, (CHUNK, CHUNK), 0)
     col = lax.broadcasted_iota(jnp.int32, (CHUNK, CHUNK), 1)
-    rates = jnp.concatenate([decay[j * CHUNK : (j + 1) * CHUNK, :].T for j in range(chunks)], axis=0)
+    rates = jnp.concatenate([decay[:, j * CHUNK : (j + 1) * CHUNK] for j in range(chunks)], axis=0)
     cumulative = exact_dot(rates, (row <= col).astype(F32))
     ending = exact_dot(rates, jnp.ones((CHUNK, CHUNK), F32))
     grow[...] = jnp.exp(cumulative)
@@ -101,15 +101,13 @@
     shrink[...] = jnp.exp(-cumulative).T
 
     def local_state(h):
-        load(k_hbm, k, k_sem, h).wait()
-        load(v_hbm, v, v_sem, h).wait()
         total = jnp.zeros((HD, HD), F32)
         for j in range(chunks):
             rows = slice(j * CHUNK, (j + 1) * CHUNK)
             at = pl.ds(j * heads + h, 1)
             starts[h, j, 0:HD, :], starts[h, j, HD : 2 * HD, :] = two_terms(total)
-            keys = k[h, rows, :].astype(F32).T * fade[at, :]
-            values = v[h, rows, :]
+            keys = k[rows, columns(h)].astype(F32).T * fade[at, :]
+            values = v[rows, columns(h)]
             added = jnp.dot(
                 jnp.concatenate(two_terms(keys), axis=1),
                 jnp.concatenate([values, values], axis=0),
@@ -130,19 +128,54 @@
         total = y_got[h, 0]
         for y in range(1, ny):
             total = total * jnp.exp(-end_y[y, pl.ds(h, 1), :]) + y_got[h, y]
+        return total
+
+    def send_z(h):
+        total = group_total(h)
         z_own[h] = total
         z_got[h, my_z] = total
         for i in range(1, nz):
             device = z_peer(i)[1]
-            remote(z_own.at[h], z_got.at[h, my_z], z_send, z_recv.at[h], device).start()
-
-    def hand_back(h):
+            remote(z_own.at[h], z_got.at[h, my_z], z_send.at[h], z_recv.at[h], device).start()
+
+    def z_sent(h):
+        wait_for(z_got.at[h, pl.ds(0, nz - 1)], z_send.at[h])
+
+    def group_rows(z):
+        return pl.ds(pl.multiple_of(z * share, share), share)
+
+    def send_group():
+        group_got[my_z] = group[group_rows(my_z), :]
+        for i in range(1, nz):
+            other, device = z_peer(i)
+            remote(group.at[group_rows(other)], group_got.at[my_z], g_send, g_recv, device).start()
+
+    def scan_group():
+        wait_for(group_got.at[pl.ds(0, nz - 1)], g_recv)
+        h = DIRECT + (my_z * share) // piece
+        total = jnp.zeros((share, HD), F32)
+        for z in range(nz):
+            group_back[z] = total
+            if z + 1 < nz:
+                total = total * jnp.exp(-end_z[z, pl.ds(h, 1), :]) + group_got[z]
+        mine = group_rows(my_z)
+        group_in[mine, :] = group_back[my_z]
+        for i in range(1, nz):
+            other, device = z_peer(i)
+            remote(group_back.at[other], group_in.at[mine], gb_send, gb_recv, device).start()
+
+    def direct_before(h):
         wait_for(z_got.at[h, pl.ds(0, nz - 1)], z_recv.at[h])
 
         def add(z, total):
             return total * jnp.exp(-end_z[z, pl.ds(h, 1), :]) + z_got[h, z]
 
-        total = lax.fori_loop(0, my_z, add, jnp.zeros((piece, HD), F32))
+        return lax.fori_loop(0, my_z, add, jnp.zeros((piece, HD), F32))
+
+    def group_before(h):
+        return group_in[pl.ds(pl.multiple_of((h - DIRECT) * piece, piece), piece), :]
+
+    def hand_back(h, total):
         for y in range(ny):
             back[h, y] = total
             if y + 1 < ny:
@@ -154,12 +187,11 @@
             remote(back.at[h, other], incoming.at[h, mine], b_send, b_recv.at[h], device).start()
 
     def within(h):
-        load(q_hbm, q, q_sem, h).wait()
         causal = row >= col
         for j in range(chunks):
             rows = slice(j * CHUNK, (j + 1) * CHUNK)
             at = pl.ds(j * heads + h, 1)
-            queries, keys, values = q[h, rows, :], k[h, rows, :], v[h, rows, :]
+            queries, keys, values = q[rows, columns(h)], k[rows, columns(h)], v[rows, columns(h)]
             scores = lax.dot_general(queries, keys, (((1,), (1,)), ((), ())), preferred_element_type=F32)
             weights = jnp.where(causal, scores * grow[at, :], 0.0)
             inner[h, rows, :] = jnp.dot(
@@ -173,14 +205,14 @@
     def finish(h):
         wait_for(incoming.at[h, pl.ds(0, (ny - 1) * piece)], b_recv.at[h])
         entering = jnp.concatenate(two_terms(incoming[h]), axis=0)
-        gain = gain_ref[pl.ds(h, 1), :]
+        gain = gains[pl.ds(h, 1), :]
         target = pl.ds(pl.multiple_of((head_at * heads + h) * HD, HD), HD)
         lane = lax.broadcasted_iota(jnp.int32, (CHUNK, chunks * heads), 1)
         for i in range(1, chunks + 1):
             j, device = x_peer(i)
             rows = pl.ds(pl.multiple_of(j * CHUNK, CHUNK), CHUNK)
             at = j * heads + h
-            queries = q[h, rows, :]
+            queries = q[rows, columns(h)]
             carried = jnp.dot(
                 jnp.concatenate([queries, queries], axis=1), entering, preferred_element_type=F32
             )
@@ -193,13 +225,15 @@
             else:
                 pltpu.make_async_copy(normed.at[h, j], out_hbm.at[:, target], own_sem.at[h]).start()
 
+    k_copy.wait()
+    v_copy.wait()
     local_state(0)
     pl.semaphore_wait(barrier, ny + nz + chunks - 3)
     for i in range(1, ny):
         remote(end_y.at[my_y], end_y.at[my_y], end_send, end_y_recv, y_peer(i)[1]).start()
     send_y(0)
 
-    @pl.loop(1, heads)
+    @pl.loop(1, DIRECT)
     def _(h):
         local_state(h)
         send_y(h)
@@ -212,30 +246,68 @@
     end_z[my_z] = group_end
     for i in range(1, nz):
         remote(end_z_own, end_z.at[my_z], end_send, end_z_recv, z_peer(i)[1]).start()
-
-    @pl.loop(0, heads)
-    def _(h):
-        group_total(h)
-
+    send_z(0)
+
+    @pl.loop(DIRECT, heads)
+    def _(h):
+        local_state(h)
+        send_y(h)
+
+    z_sent(0)
+    send_z(1)
+
+    @pl.loop(DIRECT, heads)
+    def _(h):
+        group[pl.ds(pl.multiple_of((h - DIRECT) * piece, piece), piece), :] = group_total(h)
+
+    send_group()
+    q_copy.wait()
     within(0)
+    z_sent(1)
+    send_z(2)
+    within(1)
+    gain_copy.wait()
     wait_for(end_z.at[pl.ds(0, nz - 1)], end_z_recv)
-    hand_back(0)
-
-    @pl.loop(1, heads)
-    def _(h):
-        within(h)
-        hand_back(h)
+    hand_back(0, direct_before(0))
+    z_sent(2)
+    send_z(3)
+    within(2)
+    hand_back(1, direct_before(1))
+    finish(0)
+    scan_group()
+
+    @pl.loop(2, DIRECT)
+    def _(h):
+        within(h + 1)
+        hand_back(h, direct_before(h))
         finish(h - 1)
+
+    wait_for(group_in.at[pl.ds(0, (nz - 1) * share)], gb_recv)
+
+    @pl.loop(DIRECT, heads)
+    def _(h):
+        hand_back(h, group_before(h))
+
+    @pl.loop(DIRECT, heads)
+    def _(h):
+        finish(h - 1)
+
+        @pl.when(h + 1 < heads)
+        def _():
+            within(h + 1)
 
     finish(heads - 1)
 
     wait_for(end_y.at[pl.ds(0, ny - 1)], end_send)
     wait_for(end_z.at[pl.ds(0, nz - 1)], end_send)
+    wait_for(group_got.at[pl.ds(0, nz - 1)], g_send)
+    wait_for(group_got.at[pl.ds(0, nz - 1)], gb_send)
+
+    z_sent(DIRECT - 1)
 
     @pl.loop(0, heads)
     def _(h):
         wait_for(y_got.at[h, pl.ds(0, ny - 1)], y_send)
-        wait_for(z_got.at[h, pl.ds(0, nz - 1)], z_send)
         wait_for(back.at[h, pl.ds(0, ny - 1)], b_send)
         wait_for(normed.at[h, pl.ds(0, chunks - 1)], x_send)
         target = pl.ds(pl.multiple_of((head_at * heads + h) * HD, HD), HD)
@@ -251,18 +323,20 @@
     nz = lax.axis_size("seq") // ny
     piece = HD // ny
     rows = chunks * heads
-    any_space = pl.BlockSpec(memory_space=pl.ANY)
+    share = (heads - DIRECT) * piece // nz
+    in_hbm = pl.BlockSpec(memory_space=pltpu.HBM)
     dma = pltpu.SemaphoreType.DMA
     return pl.pallas_call(
         functools.partial(kernel, (heads, chunks, ny, nz)),
-        out_shape=jax.ShapeDtypeStruct((CHUNK, chunks * width), BF16),
-        in_specs=[any_space] * 4 + [pl.BlockSpec(memory_space=pltpu.VMEM)],
-        out_specs=any_space,
+        out_shape=pltpu.VMEM((CHUNK, chunks * width), BF16),
+        in_specs=[in_hbm] * 5,
+        out_specs=pl.BlockSpec(memory_space=pltpu.VMEM),
         scratch_shapes=[
-            pltpu.VMEM((heads, tokens, HD), BF16),
-            pltpu.VMEM((heads, tokens, HD), BF16),
-            pltpu.VMEM((heads, tokens, HD), BF16),
-            pltpu.VMEM((tokens, heads), F32),
+            pltpu.VMEM((tokens, width), BF16),
+            pltpu.VMEM((tokens, width), BF16),
+            pltpu.VMEM((tokens, width), BF16),
+            pltpu.VMEM((heads, tokens), F32),
+            pltpu.VMEM((heads, HD), F32),
             pltpu.VMEM((rows, CHUNK), F32),
             pltpu.VMEM((rows, CHUNK), F32),
             pltpu.VMEM((rows, CHUNK), F32),
@@ -272,23 +346,27 @@
             pltpu.VMEM((heads, chunks, 2 * HD, HD), BF16),
             pltpu.VMEM((heads, tokens, HD), F32),
             pltpu.VMEM((heads, ny, piece, HD), F32),
-            pltpu.VMEM((heads, piece, HD), F32),
-            pltpu.VMEM((heads, nz, piece, HD), F32),
+            pltpu.VMEM((DIRECT, piece, HD), F32),
+            pltpu.VMEM((DIRECT, nz, piece, HD), F32),
             pltpu.VMEM((heads, ny, piece, HD), F32),
             pltpu.VMEM((heads, HD, HD), F32),
             pltpu.VMEM((heads, chunks, CHUNK, HD), BF16),
+            pltpu.VMEM((nz * share, HD), F32),
+            pltpu.VMEM((nz, share, HD), F32),
+            pltpu.VMEM((nz, share, HD), F32),
+            pltpu.VMEM((nz * share, HD), F32),
             pltpu.VMEM((ny, heads, HD), F32),
             pltpu.VMEM((heads, HD), F32),
             pltpu.VMEM((nz, heads, HD), F32),
-            dma, dma((heads,)), dma((heads,)), dma((heads,)),
-            dma, dma, dma, dma, dma((heads,)), dma, dma((heads,)), dma, dma((heads,)), dma, dma,
-            dma((heads,)),
+            dma, dma, dma, dma, dma,
+            dma, dma, dma, dma, dma((heads,)), dma((DIRECT,)), dma((DIRECT,)), dma, dma((heads,)), dma, dma,
+            dma((heads,)), dma, dma, dma, dma,
         ],
         compiler_params=pltpu.CompilerParams(
-            collective_id=0, has_side_effects=True, vmem_limit_bytes=52 * 2**20
+            collective_id=0, has_side_effects=True, vmem_limit_bytes=60 * 2**20
         ),
         name="lightning",
-    )(lin_query, lin_key, lin_value, log_decay, norm_gain.reshape(heads, HD))
+    )(lin_query, lin_key, lin_value, log_decay.T, norm_gain.reshape(heads, HD))
 
 
 def solution(mesh):

time: 58.5 us -> 53.5 us (0.915)
  local copies, waits for them, and re-layouts: 4.73 us -> 1.32 us
  Pallas kernels: 53.5 us -> 52.1 us
    unnamed x4 -> x1, local copies, waits for them, and re-layouts: 4.73 us -> 1.32 us
    pallas_call x1, Pallas kernels: 53.5 us -> 52.1 us  [on_device(): pl.pallas_call(functools.partial(kernel, (heads, chunks, ny, nz)), out_sh...]
where the time goes in v2:
time: 53.5 us; the launch traced here: 53.4 us
  Pallas kernels  52.1 us (97%)
  local copies, waits for them, and re-layouts  1.32 us (2%)
    pallas_call x1, Pallas kernels, on_device(): pl.pallas_call(functools.partial(kernel, (heads, chunks, ny, nz)), out_sh...  52.1 us
    unnamed x1, local copies, waits for them, and re-layouts  1.32 us

profile of v2, /device:TPU:1, one launch (start us, length us, event | category | flops | bytes accessed | tf_op | source)
XLA Modules:
  0.0 53.4 jit_solution(15495362490993647962)
XLA Ops:
  0.0 52.1 %lightning.1 = bf16[128,8192]{1,0:T(8,128)(2,1)S(1)} custom-call(bf16[1024,1024]{1,0:T(8,128)(2,1)} %q_hbm.1, bf16[1024,1024]{1,0:T(8,128)(2,1)} %k_hbm.1, bf16[1024,1024]{1,0:T(8,128)(2,1)} %v_hbm.1, f32[8,1024]{1,0:T(8,128)} %bitcast.2, f32[8,128]{1,0:T(8,128)} %bitcast.3), custom_call_target="tpu_custom_call" | custom-call | tf_op jit(solution)/shard_map/lightning/pallas_call | solution.py:329
  52.1 1.3 %copy.7 = bf16[128,8192]{1,0:T(8,128)(2,1)} copy(bf16[128,8192]{1,0:T(8,128)(2,1)S(1)} %lightning.1) | data formatting | bytes 4194304

commit v3 on v2

--- a/solution.py
+++ b/solution.py
@@ -75,7 +75,6 @@
     v_copy = pltpu.make_async_copy(v_hbm, v, v_sem)
     v_copy.start()
     q_copy = pltpu.make_async_copy(q_hbm, q, q_sem)
-    q_copy.start()
     barrier = pltpu.get_barrier_semaphore()
     for i in range(1, ny):
         pl.semaphore_signal(barrier, inc=1, device_id=y_peer(i)[1], device_id_type=MESH)
@@ -89,16 +88,15 @@
     col = lax.broadcasted_iota(jnp.int32, (CHUNK, CHUNK), 1)
     rates = jnp.concatenate([decay[:, j * CHUNK : (j + 1) * CHUNK] for j in range(chunks)], axis=0)
     cumulative = exact_dot(rates, (row <= col).astype(F32))
-    ending = exact_dot(rates, jnp.ones((CHUNK, CHUNK), F32))
-    grow[...] = jnp.exp(cumulative)
+    ending = jnp.broadcast_to(cumulative[:, CHUNK - 1 :], cumulative.shape)
     fade[...] = jnp.exp(cumulative - ending)
     chunk_fade[...] = jnp.exp(-ending)
     so_far = jnp.zeros((heads, HD), F32)
     for j in range(chunks):
-        start_fade[j * heads : (j + 1) * heads, :] = jnp.exp(-so_far)
+        start_fade[j * heads : (j + 1) * heads, :] = so_far
         so_far = so_far + ending[j * heads : (j + 1) * heads, :]
     end_y[my_y] = so_far
-    shrink[...] = jnp.exp(-cumulative).T
+    grow[...] = cumulative
 
     def local_state(h):
         total = jnp.zeros((HD, HD), F32)
@@ -227,6 +225,7 @@
 
     k_copy.wait()
     v_copy.wait()
+    q_copy.start()
     local_state(0)
     pl.semaphore_wait(barrier, ny + nz + chunks - 3)
     for i in range(1, ny):
@@ -262,6 +261,9 @@
 
     send_group()
     q_copy.wait()
+    start_fade[...] = jnp.exp(-start_fade[...])
+    shrink[...] = jnp.exp(-grow[...]).T
+    grow[...] = jnp.exp(grow[...])
     within(0)
     z_sent(1)
     send_z(2)
@@ -274,13 +276,14 @@
     within(2)
     hand_back(1, direct_before(1))
     finish(0)
+
+    within(3)
+    hand_back(2, direct_before(2))
     scan_group()
-
-    @pl.loop(2, DIRECT)
-    def _(h):
-        within(h + 1)
-        hand_back(h, direct_before(h))
-        finish(h - 1)
+    finish(1)
+    within(4)
+    hand_back(3, direct_before(3))
+    finish(2)
 
     wait_for(group_in.at[pl.ds(0, (nz - 1) * share)], gb_recv)
 

time: 53.5 us -> 53.5 us (level)
  no operation moved by 1% of the time
where the time goes in v3:
time: 53.5 us; the launch traced here: 53.4 us
  Pallas kernels  52.1 us (97%)
  local copies, waits for them, and re-layouts  1.32 us (2%)
    pallas_call x1, Pallas kernels, on_device(): pl.pallas_call(functools.partial(kernel, (heads, chunks, ny, nz)), out_sh...  52.1 us
    unnamed x1, local copies, waits for them, and re-layouts  1.32 us

profile of v3, /device:TPU:1, one launch (start us, length us, event | category | flops | bytes accessed | tf_op | source)
XLA Modules:
  0.0 53.4 jit_solution(11191205309016276609)
XLA Ops:
  0.0 52.1 %lightning.1 = bf16[128,8192]{1,0:T(8,128)(2,1)S(1)} custom-call(bf16[1024,1024]{1,0:T(8,128)(2,1)} %q_hbm.1, bf16[1024,1024]{1,0:T(8,128)(2,1)} %k_hbm.1, bf16[1024,1024]{1,0:T(8,128)(2,1)} %v_hbm.1, f32[8,1024]{1,0:T(8,128)} %bitcast.2, f32[8,128]{1,0:T(8,128)} %bitcast.3), custom_call_target="tpu_custom_call" | custom-call | tf_op jit(solution)/shard_map/lightning/pallas_call | solution.py:332
  52.1 1.3 %copy.7 = bf16[128,8192]{1,0:T(8,128)(2,1)} copy(bf16[128,8192]{1,0:T(8,128)(2,1)S(1)} %lightning.1) | data formatting | bytes 4194304
